TPU v7x, 32 devices: a whole 2x2x4 slice. The times are simulated.
32 devices in a mesh: dp: 4 (over y, x), shard: 8 (over z, core).
Axes of the slice: x: 2, y: 2, z: 4, core: 2. Of those that a mesh axis runs over, the one named last changes fastest.
Arguments:
- hot_ids: int32 [4096, 8], P(('dp', 'shard')), may hold values from 0 to 4095
- cold_owner: int32 [8192, 1], P(('dp', 'shard')), may hold values from 0 to 7; in each aligned block of 256 rows (0 to 255, 256 to 511, ...) at most 64 rows name the same one
- cold_offset: int32 [8192], P(('dp', 'shard')), may hold values from 0 to 4095
- hot_table: bfloat16 [4096, 128], replicated, may hold values from -2 to 2
- cold_table: bfloat16 [32768, 128], P('shard'), may hold values from -4 to 4
- w_in: bfloat16 [256, 4096], P(None, 'shard'), may hold values from -0.375 to 0.375
- bias_in: bfloat16 [1, 4096], P(None, 'shard'), may hold values from -0.59765625 to 0.59765625
- w_out: bfloat16 [1, 4096], P(None, 'shard'), may hold values from -0.1875 to 0.1875
- cotangent: float32 [4096], P(('dp', 'shard')), may hold values from -10 to 10
Outputs:
- logits: float32 [4096], P(('dp', 'shard'))
- hot_grad: bfloat16 [4096, 128], P('shard')
- cold_grad: bfloat16 [32768, 128], P('shard')
- w_in_grad: float32 [256, 4096], P(None, 'shard')
Inputs may be any that keep to these rules, and one draw needn't show every extreme that they name: `cold_owner`: within the 256 cold lookups of one device no owner is named more than 64 times, a bound that some block reaches.
All inputs are finite; a program needn't handle non-finite values.
Results may differ from a plain program's by a relative error of at most 0.015.
Values may be sent and summed in bfloat16 or wider, within the bound.
A program may use at most 64 MiB of HBM per device.

v0:
```python
import jax
import jax.numpy as jnp
from jax import lax
from jax.sharding import PartitionSpec as P


def contract_rows(left, right):
    return lax.dot_general(
        left, right, (((0,), (0,)), ((), ())), preferred_element_type=jnp.float32
    )


def shards(
    hot_ids, cold_owner, cold_offset, hot_table, cold_table, w_in, bias_in, w_out, cotangent
):
    shard_count = lax.axis_size("shard")
    my_index = lax.axis_index("shard")
    samples_dev = hot_ids.shape[0]
    hot_width = hot_ids.shape[1]
    table_rows = hot_table.shape[0]
    embed = hot_table.shape[1]
    kept_rows = table_rows // shard_count
    owned_rows = cold_table.shape[0]
    row_numbers = jnp.arange(table_rows, dtype=jnp.int32)
    hot_counts = jnp.zeros((samples_dev, table_rows), jnp.float32)
    for lookup in range(hot_width):
        hot_counts = hot_counts + (hot_ids[:, lookup][:, None] == row_numbers[None, :]).astype(
            jnp.float32
        )
    hot_counts = hot_counts.astype(jnp.bfloat16)
    hot_pooled = jnp.dot(hot_counts, hot_table, preferred_element_type=jnp.float32)
    owner_ids = cold_owner[:, 0]
    lookups = owner_ids.shape[0]
    per_sample = lookups // samples_dev
    capacity = max(2, 2 * lookups // shard_count)
    matches = (owner_ids[:, None] == jnp.arange(shard_count, dtype=jnp.int32)[None, :]).astype(
        jnp.int32
    )
    ordinal = jnp.cumsum(matches, axis=0) - 1
    slot_index = jnp.sum(ordinal * matches, axis=1)
    slot_place = owner_ids * capacity + slot_index
    slot_match = slot_place[:, None] == jnp.arange(shard_count * capacity, dtype=jnp.int32)[None, :]
    requests = jnp.sum(jnp.where(slot_match, cold_offset[:, None], 0), axis=0).reshape(
        shard_count, capacity
    )
    present = jnp.sum(slot_match.astype(jnp.int32), axis=0).reshape(shard_count, capacity)
    slot_table = slot_match.astype(jnp.bfloat16)
    offsets = lax.all_to_all(requests, "shard", split_axis=0, concat_axis=0, tiled=True)
    markers = lax.all_to_all(present, "shard", split_axis=0, concat_axis=0, tiled=True)
    fetched = jnp.take(cold_table, offsets, axis=0)
    fetched = jnp.where(markers[:, :, None] > 0, fetched, jnp.zeros_like(fetched))
    answer = lax.all_to_all(fetched, "shard", split_axis=0, concat_axis=0, tiled=True)
    mine = jnp.dot(slot_table, answer.reshape(-1, embed), preferred_element_type=jnp.float32)
    cold_pooled = jnp.sum(mine.reshape(samples_dev, per_sample, embed), axis=1)
    inputs = jnp.concatenate([hot_pooled, cold_pooled], axis=1).astype(jnp.bfloat16)
    group_inputs = lax.all_gather(inputs, "shard", axis=0, tiled=True)
    preact = (
        jnp.dot(group_inputs, w_in, preferred_element_type=jnp.float32)
        + bias_in[0].astype(jnp.float32)[None, :]
    )
    sigma = jax.nn.sigmoid(preact)
    hidden = (preact * sigma).astype(jnp.bfloat16)
    logit_share = jnp.dot(hidden, w_out[0], preferred_element_type=jnp.float32)
    group_logits = lax.psum(logit_share, "shard")
    logits = lax.dynamic_slice_in_dim(group_logits, my_index * samples_dev, samples_dev, 0)
    group_cotangent = lax.all_gather(cotangent, "shard", axis=0, tiled=True)
    slope = sigma * (1.0 + preact * (1.0 - sigma))
    hidden_grad = (group_cotangent[:, None] * w_out[0].astype(jnp.float32)[None, :] * slope).astype(
        jnp.bfloat16
    )
    weight_group = contract_rows(group_inputs, hidden_grad).astype(jnp.bfloat16)
    input_grad = lax.psum_scatter(
        jnp.dot(hidden_grad, w_in.T, preferred_element_type=jnp.float32).astype(jnp.bfloat16),
        "shard",
        scatter_dimension=0,
        tiled=True,
    )
    hot_part = contract_rows(hot_counts, input_grad[:, :embed])
    hot_everywhere = lax.psum(hot_part, ("dp", "shard"))
    hot_total = lax.dynamic_slice_in_dim(hot_everywhere, my_index * kept_rows, kept_rows, 0)
    per_lookup = jnp.repeat(input_grad[:, embed:], per_sample, axis=0)
    outgoing = (
        contract_rows(slot_table, per_lookup)
        .astype(jnp.bfloat16)
        .reshape(shard_count, capacity, embed)
    )
    incoming = lax.all_to_all(outgoing, "shard", split_axis=0, concat_axis=0, tiled=True)
    offset_table = (
        offsets.reshape(-1)[:, None] == jnp.arange(owned_rows, dtype=jnp.int32)[None, :]
    ).astype(jnp.bfloat16)
    cold_part = contract_rows(offset_table, incoming.reshape(-1, embed))
    cold_total, weight_total = (
        lax.psum(cold_part.astype(jnp.bfloat16), "dp").astype(jnp.float32),
        lax.psum(weight_group, "dp").astype(jnp.float32),
    )
    return (logits, hot_total.astype(jnp.bfloat16), cold_total.astype(jnp.bfloat16), weight_total)


def solution(mesh):
    in_specs = (
        P(("dp", "shard"), None),
        P(("dp", "shard"), None),
        P(("dp", "shard")),
        P(),
        P("shard", None),
        P(None, "shard"),
        P(None, "shard"),
        P(None, "shard"),
        P(("dp", "shard")),
    )
    out_specs = (P(("dp", "shard")), P("shard", None), P("shard", None), P(None, "shard"))
    return jax.shard_map(shards, mesh=mesh, in_specs=in_specs, out_specs=out_specs, check_vma=False)
```

profile of v0, /device:TPU:0, one launch (start us, length us, event | category | flops | bytes accessed | tf_op | source)
XLA Modules:
  0.0 214.7 jit_solution(14971163135114629105)
XLA Ops:
  7.2 0.8 fusion.11
  8.0 0.6 reduce-window.6
  8.5 0.2 slice_reduce_fusion
  8.8 0.8 fusion.10
  9.6 0.5 broadcast.99
  10.1 1.3 fusion.14
  11.4 0.8 convert_reduce_fusion
  12.3 0.7 all_to_all.24
  12.9 6.3 %all-to-all-start.1 = ((s32[8,1,64]{2,1,0:T(1,128)}), s32[8,1,64]{2,1,0:T(1,128)S(1)}, u32[]{:S(2)}, u32[]{:S(2)}) async-start(s32[8,1,64]{2,1,0:T(1,128)} %all_to_all.24), calls=%async_computation.1 | async-start | bytes 8192 | tf_op jit(solution)/shard_map/all_to_all | solution.py:48
  19.3 1.0 slice_bitcast_fusion.7
  20.2 0.7 reduce.2
  20.9 0.7 add.104
  21.6 0.7 all_to_all.22
  22.3 0.1 eq.239
  22.4 0.1 copy.20
  22.5 12.3 %all-gather = f32[8,1,128]{2,1,0:T(1,128)S(1)} all-gather(f32[1,1,128]{2,1,0:T(1,128)} %bitcast.77), channel_id=1, replica_groups=mesh['dp'=4,'shard'=8] {'shard'}, dimensions={0}, use_global_device_ids=true | all-gather | bytes 4608 | tf_op jit(solution)/shard_map/all_gather | solution.py:66
  34.8 3.3 %all-to-all-start = ((s32[8,1,64]{2,1,0:T(1,128)}), s32[8,1,64]{2,1,0:T(1,128)S(1)}, u32[]{:S(2)}, u32[]{:S(2)}) async-start(s32[8,1,64]{2,1,0:T(1,128)} %all_to_all.22), calls=%async_computation | async-start | bytes 8192 | tf_op jit(solution)/shard_map/all_to_all | solution.py:49
  38.2 0.1 reshape.125
  38.3 5.3 %all-to-all-done = s32[8,1,64]{2,1,0:T(1,128)S(1)} async-done(((s32[8,1,64]{2,1,0:T(1,128)}), s32[8,1,64]{2,1,0:T(1,128)S(1)}, u32[]{:S(2)}, u32[]{:S(2)}) %all-to-all-start) | async-done | bytes 2080 | tf_op jit(solution)/shard_map/all_to_all | solution.py:49
  43.6 1.3 gather_fusion
  44.9 0.9 select_select_fusion
  45.8 3.4 %all-to-all-start.2 = ((bf16[8,64,128]{2,1,0:T(8,128)(2,1)}), bf16[8,64,128]{2,1,0:T(8,128)(2,1)S(1)}, u32[]{:S(2)}, u32[]{:S(2)}) async-start(bf16[8,64,128]{2,1,0:T(8,128)(2,1)} %select_select_fusion), calls=%async_computation.2 | async-start | bytes 262144 | tf_op jit(solution)/shard_map/all_to_all | solution.py:52
  49.2 0.0 reduce-scatter.2.cloned.1.call-start
  49.2 3.7 %convolution_convert_fusion.3 = bf16[128,128]{0,1:T(8,128)(2,1)S(1)} fusion(bf16[4096,128]{1,0:T(8,128)(2,1)} %param.12, s32[128]{0:T(128)S(1)} %get-tuple-element.16, s32[128]{0:T(128)S(1)} %get-tuple-element.17, s32[128]{0:T(128)S(1)} %get-tuple-element.11, s32[128]{0:T(128)S(1)} %get-tuple-element.12, s32[128]{0:T(128)S(1)} %get-tuple-element.13, ...), kind=kOutput, calls=%fused_computation.21 | convolution fusion | flops 146817024 | bytes 1085440 | tf_op jit(solution)/shard_map/dot_general | solution.py:31
  53.0 2.9 %all-to-all-done.2 = bf16[8,64,128]{2,1,0:T(8,128)(2,1)S(1)} async-done(((bf16[8,64,128]{2,1,0:T(8,128)(2,1)}), bf16[8,64,128]{2,1,0:T(8,128)(2,1)S(1)}, u32[]{:S(2)}, u32[]{:S(2)}) %all-to-all-start.2) | async-done | bytes 131104 | tf_op jit(solution)/shard_map/all_to_all | solution.py:52
  55.9 0.3 convolution_reduce_fusion
  56.1 0.1 copy.22
  56.3 14.0 %all_gather.6 = bf16[1024,256]{0,1:T(8,128)(2,1)S(1)} all-gather(bf16[128,256]{0,1:T(8,128)(2,1)S(1)} %pad_maximum_fusion), channel_id=1, replica_groups=mesh['dp'=4,'shard'=8] {'shard'}, dimensions={0}, use_global_device_ids=true | all-gather | bytes 589824 | tf_op jit(solution)/shard_map/all_gather | solution.py:56
  70.3 2.3 %multiply_convert_fusion = (bf16[1024,512]{1,0:T(8,128)(2,1)S(1)}, f32[1024,512]{1,0:T(8,128)}) fusion(f32[512]{0:T(512)S(1)} %mul.50, f32[1024]{0:T(1024)S(1)} %bitcast.70, f32[512]{0:T(512)S(1)} %bitcast.75, bf16[1024,256]{0,1:T(8,128)(2,1)S(1)} %all_gather.6, bf16[256,512]{1,0:T(8,128)(2,1)S(1)} %copy-done.1), kind=kOutput, calls=%fused_computation.5 | convolution fusion | flops 274202624 | bytes 3940352 | tf_op jit(solution)/shard_map/dot_general | solution.py:58
  72.6 1.3 convolution_convert_fusion
  73.9 0.7 reduce.10
  74.5 0.1 eq.248
  74.6 28.9 %reduce-scatter.2.cloned.1.call-done = bf16[128,256]{1,0:T(8,128)(2,1)} async-done(((bf16[1024,256]{1,0:T(8,128)(2,1)}), bf16[128,256]{1,0:T(8,128)(2,1)}) %reduce-scatter.2.cloned.1.call-update) | async-done | bytes 65552 | tf_op jit(solution)/shard_map/reduce_scatter | solution.py:72
  103.5 0.8 slice.52
  104.3 1.1 convolution_convert_fusion.2
  105.4 3.4 %all-to-all-start.3 = ((bf16[8,64,128]{2,1,0:T(8,128)(2,1)}), bf16[8,64,128]{2,1,0:T(8,128)(2,1)S(1)}, u32[]{:S(2)}, u32[]{:S(2)}) async-start(bf16[8,64,128]{2,1,0:T(8,128)(2,1)} %bitcast.27), calls=%async_computation.4 | async-start | bytes 262144 | tf_op jit(solution)/shard_map/all_to_all | solution.py:87
  108.8 0.0 all-reduce.4.cloned.1.call-start
  108.8 1.2 convolution_convert_fusion.1
  110.0 5.5 %all-to-all-done.3 = bf16[8,64,128]{2,1,0:T(8,128)(2,1)S(1)} async-done(((bf16[8,64,128]{2,1,0:T(8,128)(2,1)}), bf16[8,64,128]{2,1,0:T(8,128)(2,1)S(1)}, u32[]{:S(2)}, u32[]{:S(2)}) %all-to-all-start.3) | async-done | bytes 131104 | tf_op jit(solution)/shard_map/all_to_all | solution.py:87
  115.5 3.4 %fusion.1 = bf16[4096,128]{1,0:T(8,128)(2,1)} fusion(bf16[512,128]{1,0:T(8,128)(2,1)S(1)} %bitcast.62, s32[512]{0:T(512)S(1)} %eq.248), kind=kOutput, calls=%fused_computation.3 | convolution fusion | flops 539492352 | bytes 1181696 | tf_op jit(solution)/shard_map/dot_general | solution.py:8
  118.9 2.3 %fusion.3 = f32[1,1024]{1,0:T(1,128)S(1)} fusion(f32[1024,512]{1,0:T(8,128)} %get-tuple-element.19, f32[512]{0:T(512)S(1)} %bitcast.76, bf16[1,512]{1,0:T(2,128)(2,1)S(1)} %copy-done.3), kind=kOutput, calls=%fused_computation.22 | convolution fusion | flops 4194304 | bytes 2104320 | tf_op jit(solution)/shard_map/dot_general | solution.py:63
  121.2 14.4 %psum.28 = f32[1024]{0:T(1024)S(1)} all-reduce(f32[1024]{0:T(1024)S(1)} %bitcast.71), channel_id=1, replica_groups=mesh['dp'=4,'shard'=8] {'shard'}, use_global_device_ids=true, to_apply=%region_6.7 | all-reduce | flops 1024 | bytes 8192 | tf_op jit(solution)/shard_map/psum | solution.py:64
  135.6 0.6 dynamic_slice.6
  136.2 2.3 %fusion.6 = f32[4096,128]{1,0:T(8,128)S(1)} fusion(s32[128]{0:T(128)S(1)} %get-tuple-element.16, s32[128]{0:T(128)S(1)} %get-tuple-element.17, s32[128]{0:T(128)S(1)} %get-tuple-element.11, s32[128]{0:T(128)S(1)} %get-tuple-element.12, s32[128]{0:T(128)S(1)} %get-tuple-element.13, s32[128]{0:T(128)S(1)} %get-tuple-element.14, ...), kind=kOutput, calls=%fused_computation.28 | convolution fusion | flops 146800640 | bytes 2134016 | tf_op jit(solution)/shard_map/dot_general | solution.py:8
  138.6 63.7 %all-reduce.5 = bf16[4096,128]{1,0:T(8,128)(2,1)} all-reduce(f32[4096,128]{1,0:T(8,128)S(1)} %fusion.6), channel_id=1, replica_groups=mesh['dp'=4,'shard'=8] {'dp','shard'}, use_global_device_ids=true, to_apply=%region_8.9 | all-reduce | flops 524288 | bytes 3145728 | tf_op jit(solution)/shard_map/psum | solution.py:79
  202.3 1.6 dynamic-slice_convert_fusion
  203.8 1.8 convert_element_type.86
  205.6 2.3 %copy.27 = bf16[4096,128]{1,0:T(8,128)(2,1)} copy(bf16[4096,128]{1,0:T(8,128)(2,1)} %get-tuple-element.22) | data formatting | bytes 2097152
  (21 shorter events, 0.2 us)
Async XLA Ops:
  7.2 36.4 %copy-start = (bf16[4096,128]{1,0:T(8,128)(2,1)S(1)}, bf16[4096,128]{1,0:T(8,128)(2,1)}, u32[]{:S(2)}) copy-start(bf16[4096,128]{1,0:T(8,128)(2,1)} %param.13) | copy-start | bytes 3145732
  12.9 21.9 %all-to-all-start.1 = ((s32[8,1,64]{2,1,0:T(1,128)}), s32[8,1,64]{2,1,0:T(1,128)S(1)}, u32[]{:S(2)}, u32[]{:S(2)}) async-start(s32[8,1,64]{2,1,0:T(1,128)} %all_to_all.24), calls=%async_computation.1 | async-start | bytes 8192 | tf_op jit(solution)/shard_map/all_to_all | solution.py:48
  34.8 8.7 %all-to-all-start = ((s32[8,1,64]{2,1,0:T(1,128)}), s32[8,1,64]{2,1,0:T(1,128)S(1)}, u32[]{:S(2)}, u32[]{:S(2)}) async-start(s32[8,1,64]{2,1,0:T(1,128)} %all_to_all.22), calls=%async_computation | async-start | bytes 8192 | tf_op jit(solution)/shard_map/all_to_all | solution.py:49
  45.8 10.1 %all-to-all-start.2 = ((bf16[8,64,128]{2,1,0:T(8,128)(2,1)}), bf16[8,64,128]{2,1,0:T(8,128)(2,1)S(1)}, u32[]{:S(2)}, u32[]{:S(2)}) async-start(bf16[8,64,128]{2,1,0:T(8,128)(2,1)} %select_select_fusion), calls=%async_computation.2 | async-start | bytes 262144 | tf_op jit(solution)/shard_map/all_to_all | solution.py:52
  49.2 54.3 %reduce-scatter.2.cloned.1.call-start = ((), (), s32[]{:S(2)}) async-start(), calls=%async_computation.5 | async-start | bytes 589824 | tf_op jit(solution)/shard_map/reduce_scatter | solution.py:72
  49.2 21.1 %copy-start.1 = (bf16[256,512]{1,0:T(8,128)(2,1)S(1)}, bf16[256,512]{1,0:T(8,128)(2,1)}, u32[]{:S(2)}) copy-start(bf16[256,512]{1,0:T(8,128)(2,1)} %param.14) | copy-start | bytes 786436
  105.4 10.1 %all-to-all-start.3 = ((bf16[8,64,128]{2,1,0:T(8,128)(2,1)}), bf16[8,64,128]{2,1,0:T(8,128)(2,1)S(1)}, u32[]{:S(2)}, u32[]{:S(2)}) async-start(bf16[8,64,128]{2,1,0:T(8,128)(2,1)} %bitcast.27), calls=%async_computation.4 | async-start | bytes 262144 | tf_op jit(solution)/shard_map/all_to_all | solution.py:87
  108.8 95.1 %all-reduce.4.cloned.1.call-start = ((), (), s32[]{:S(2)}) async-start(), calls=%async_computation.6 | async-start | bytes 2621440 | tf_op jit(solution)/shard_map/psum | solution.py:93
  115.5 3.4 %copy-start.3 = (bf16[1,512]{1,0:T(2,128)(2,1)S(1)}, bf16[1,512]{1,0:T(2,128)(2,1)}, u32[]{:S(2)}) copy-start(bf16[1,512]{1,0:T(2,128)(2,1)} %param.16) | copy-start | bytes 3076
  118.9 17.3 %copy-start.2 = (bf16[128,256]{1,0:T(8,128)(2,1)S(1)}, bf16[128,256]{1,0:T(8,128)(2,1)}, u32[]{:S(2)}) copy-start(bf16[128,256]{1,0:T(8,128)(2,1)} %reduce-scatter.2.cloned.1.call-done) | copy-start | bytes 196612
Sparse Core Ops, SparseCore 0:
  74.0 29.4 reduce-scatter.1
  119.0 61.0 all-reduce.3
where the time goes:
time: 216 us; the launch traced here: 215 us
  blocking collectives  104 us (48%)
  waiting for transfers between devices  42.6 us (20%)
  matrix products  17.9 us (8%)
  starting transfers between devices  16.5 us (8%)
  between operations  14.2 us (7%)
  local copies, waits for them, and re-layouts  10.1 us (5%)
  other arithmetic  9.09 us (4%)
    psum x1, blocking collectives, shards(): hot_everywhere = lax.psum(hot_part, ('dp', 'shard'))  63.7 us
    reduce_scatter x1, waiting for transfers between devices, shards(): lax.psum_scatter(jnp.dot(hidden_grad, w_in.T, preferred_element_type=jnp....  28.9 us
    psum x1, blocking collectives, shards(): group_logits = lax.psum(logit_share, 'shard')  14.4 us
    all_gather x1, blocking collectives, shards(): group_inputs = lax.all_gather(inputs, 'shard', axis=0, tiled=True)  14 us
    all_gather x1, blocking collectives, shards(): group_cotangent = lax.all_gather(cotangent, 'shard', axis=0, tiled=True)  12.3 us
    dot_general x4, matrix products, contract_rows(): lax.dot_general(left, right, (((0,), (0,)), ((), ())), preferred_element_...  8.01 us
    all_to_all x1, starting transfers between devices, shards(): lax.all_to_all(requests, 'shard', split_axis=0, concat_axis=0, tiled=True)  6.33 us
    all_to_all x1, waiting for transfers between devices, shards(): lax.all_to_all(outgoing, 'shard', split_axis=0, concat_axis=0, tiled=True)  5.5 us
  transfers between devices with their start and end apart: 6, of which 4 were waited for; matrix products, arithmetic and copies ran while one was open for 7% of the time, Pallas kernels for 0%

commit v1 on v0

v1 whole, which is shorter than its diff:
```python
import functools

import jax
import jax.numpy as jnp
from jax import lax
from jax.experimental import pallas as pl
from jax.experimental.pallas import tpu as pltpu
from jax.sharding import PartitionSpec as P

F32, BF16, I32 = jnp.float32, jnp.bfloat16, jnp.int32
IDS, COT, HOTIN, ROWS, COLDIN, PART, LOGIT, COLDG, HOTG = range(9)
DIDS, DWEIGHT, DHOT, DCOLD = range(4)


def dot(a, b):
    return jnp.dot(a, b, preferred_element_type=F32)


def dot_nt(a, b):
    return lax.dot_general(a, b, (((1,), (1,)), ((), ())), preferred_element_type=F32)


def dot_tn(a, b):
    return lax.dot_general(a, b, (((0,), (0,)), ((), ())), preferred_element_type=F32)


def kernel(
    n, groups, cap, keep_all,
    ids_ref, hot_col, cot_ref, hot_table, cold_table, w_in, bias, w_out,
    logit_out, hot_out, cold_out, weight_out,
    idg, cotg, ing, hot_src, cold_src, pick, tri, offc, onehot, rows_src, answer,
    hot_counts, grads, part_src, part_in, logit_src, logit_in, slot_src, slot_in,
    hotg_src, hotg_in, weight_in, hot_in, gacc,
    ssem, rsem, dssem, drsem,
):
    me = lax.axis_index("shard")
    mine = lax.axis_index("dp")
    samples, width = hot_col.shape
    table_rows, embed = hot_table.shape
    owned = cold_table.shape[0]
    hidden_dev = w_in.shape[1]
    kept = hot_out.shape[0]
    group = n * samples
    slots = n * cap

    def shard_copy(phase, src, dst, peer, source):
        return pltpu.make_async_remote_copy(
            src_ref=src, dst_ref=dst, send_sem=ssem.at[phase, peer], recv_sem=rsem.at[phase, source],
            device_id={"shard": peer}, device_id_type=pl.DeviceIdType.MESH,
        )

    def dp_copy(phase, src, dst, peer, source):
        return pltpu.make_async_remote_copy(
            src_ref=src, dst_ref=dst, send_sem=dssem.at[phase, peer], recv_sem=drsem.at[phase, source],
            device_id={"dp": peer}, device_id_type=pl.DeviceIdType.MESH,
        )

    def peers(body, count=n, own=None):
        own = me if own is None else own

        def step(i, carry):
            body(lax.rem(own + count - i, count))
            return carry

        lax.fori_loop(1, count, step, 0)

    def dp_peers(body):
        peers(body, groups, mine)

    barrier = pltpu.get_barrier_semaphore()
    peers(lambda j: pl.semaphore_signal(
        barrier, inc=1, device_id={"shard": j}, device_id_type=pl.DeviceIdType.MESH))
    dp_peers(lambda j: pl.semaphore_signal(
        barrier, inc=1, device_id={"dp": j}, device_id_type=pl.DeviceIdType.MESH))
    pl.semaphore_wait(barrier, n - 1 + groups - 1)

    def send_ids(j):
        shard_copy(IDS, ids_ref, idg.at[mine, me], j, me).start()
        shard_copy(COT, cot_ref, cotg.at[me], j, me).start()

    peers(send_ids)
    idg[mine, me] = ids_ref[...]
    cotg[me] = cot_ref[...]

    chunk = min(512, table_rows)
    pooled = jnp.zeros((samples, embed), F32)
    lane = lax.broadcasted_iota(I32, (samples, chunk), 1)
    for c in range(table_rows // chunk):
        count = jnp.zeros((samples, chunk), F32)
        for k in range(width):
            count = count + jnp.where(hot_col[:, k : k + 1] - c * chunk == lane, 1.0, 0.0)
        pooled = pooled + dot(count.astype(BF16), hot_table[c * chunk : (c + 1) * chunk, :])
    hot_src[...] = pooled.astype(BF16)
    peers(lambda j: shard_copy(HOTIN, hot_src, ing.at[me, :, pl.ds(0, embed)], j, me).start())
    ing[me, :, 0:embed] = hot_src[...]

    lookups = 2 * samples
    row_i = lax.broadcasted_iota(I32, (lookups, lookups), 0)
    col_i = lax.broadcasted_iota(I32, (lookups, lookups), 1)
    tri[...] = jnp.where(row_i < col_i, 1.0, 0.0).astype(BF16)

    def lookup_rows(block, first):
        return jnp.concatenate([block[first : first + 1], block[first + 1 : first + 2]], axis=1)

    own_block = ids_ref[...]
    owner = lookup_rows(own_block, width)
    match = jnp.where(lax.broadcasted_iota(I32, (n, lookups), 0) == owner, 1.0, 0.0)
    order = dot(match.astype(BF16), tri[...])
    place = owner * cap + jnp.sum(match * order, axis=0, keepdims=True).astype(I32)
    slot_i = lax.broadcasted_iota(I32, (slots, samples), 0)
    pick[...] = (
        jnp.where(slot_i == place[:, :samples], 1.0, 0.0)
        + jnp.where(slot_i == place[:, samples:], 1.0, 0.0)
    ).astype(BF16)

    cap_i = lax.broadcasted_iota(I32, (cap, lookups), 0)

    def fill(d, place_at):
        def one(j, carry):
            block = idg[d, j]
            hit = jnp.where(lookup_rows(block, width) == me, 1.0, 0.0)
            spread = jnp.broadcast_to(hit, (16, lookups))
            position = dot(spread.astype(BF16), tri[...])[0:1].astype(I32)
            chosen = jnp.where(cap_i == position, hit, 0.0).astype(BF16)
            offset = lookup_rows(block, width + 2)
            high = jnp.broadcast_to((offset >> 6).astype(F32), (embed, lookups)).astype(BF16)
            low = jnp.broadcast_to((offset & 63).astype(F32), (embed, lookups)).astype(BF16)
            found = dot_nt(chosen, high) * 64.0 + dot_nt(chosen, low)
            offc[pl.ds(pl.multiple_of(j * cap, cap), cap), :] = found.astype(I32)
            return carry

        lax.fori_loop(0, n, one, 0)
        lanes = lax.broadcasted_iota(I32, (slots, embed), 1)
        for c in range(owned // embed):
            onehot[place_at, :, c * embed : (c + 1) * embed] = jnp.where(
                offc[...] - c * embed == lanes, 1.0, 0.0
            ).astype(BF16)

    peers(lambda j: shard_copy(IDS, ids_ref, idg.at[mine, j], j, j).wait_recv())
    dp_peers(lambda d: dp_copy(DIDS, idg.at[mine], idg.at[mine], d, mine).start())
    at = mine if keep_all else 0
    fill(mine, at)
    rows_src[...] = dot(onehot[at], cold_table[...]).astype(BF16).reshape(n, cap, embed)
    peers(lambda j: shard_copy(ROWS, rows_src.at[j], answer.at[me], j, me).start())
    answer[me] = rows_src[me]

    kept_i = lax.broadcasted_iota(I32, (kept, samples), 0) + me * kept
    for j in range(n):
        count = jnp.zeros((kept, samples), F32)
        for k in range(width):
            count = count + jnp.where(idg[mine, j, k : k + 1, :] == kept_i, 1.0, 0.0)
        hot_counts[:, j * samples : (j + 1) * samples] = count.astype(BF16)

    peers(lambda j: shard_copy(ROWS, rows_src.at[j], answer.at[j], j, j).wait_recv())
    cold_src[...] = dot_tn(pick[...], answer[...].reshape(slots, embed)).astype(BF16)
    peers(lambda j: shard_copy(COLDIN, cold_src, ing.at[me, :, pl.ds(embed, embed)], j, me).start())
    ing[me, :, embed : 2 * embed] = cold_src[...]

    head_rows = jnp.broadcast_to(w_out[...], (16, hidden_dev))

    def dense(i, carry):
        j = lax.rem(me + i, n)

        @pl.when(i > 0)
        def _():
            shard_copy(HOTIN, hot_src, ing.at[j, :, pl.ds(0, embed)], j, j).wait_recv()
            shard_copy(COLDIN, cold_src, ing.at[j, :, pl.ds(embed, embed)], j, j).wait_recv()
            shard_copy(COT, cot_ref, cotg.at[j], j, j).wait_recv()

        pre = dot(ing[j], w_in[...]) + bias[...].astype(F32)
        sigma = jax.nn.sigmoid(pre)
        hidden = (pre * sigma).astype(BF16)
        logit_src[j] = dot_nt(head_rows, hidden)[0:8]
        cot = jnp.broadcast_to(cotg[j][0:1], (samples, samples)).T
        cot = jnp.concatenate([cot] * (hidden_dev // samples), axis=1)
        slope = sigma * (1.0 + pre * (1.0 - sigma))
        grad = (cot * w_out[...].astype(F32) * slope).astype(BF16)
        grads[j] = grad
        part_src[j] = dot_nt(grad, w_in[...]).astype(BF16)

        @pl.when(i > 0)
        def _():
            shard_copy(PART, part_src.at[j], part_in.at[me], j, me).start()
            shard_copy(LOGIT, logit_src.at[j], logit_in.at[me], j, me).start()

        return carry

    lax.fori_loop(0, n, dense, 0)
    part_in[me] = part_src[me]
    logit_in[me] = logit_src[me]

    weight_in[mine] = dot_tn(
        ing[...].reshape(group, 2 * embed), grads[...].reshape(group, hidden_dev)
    ).astype(BF16)
    dp_peers(lambda d: dp_copy(DWEIGHT, weight_in.at[mine], weight_in.at[mine], d, mine).start())

    def add_part(i, total):
        j = lax.rem(me + i, n)

        @pl.when(i > 0)
        def _():
            shard_copy(PART, part_src.at[j], part_in.at[j], j, j).wait_recv()

        return total + part_in[j].astype(F32)

    total = lax.fori_loop(0, n, add_part, jnp.zeros((samples, 2 * embed), F32))
    total = total.astype(BF16)
    hotg_src[...] = total[:, 0:embed]
    slot_src[...] = dot(pick[...], total[:, embed:]).astype(BF16).reshape(n, cap, embed)

    def send_grads(j):
        shard_copy(COLDG, slot_src.at[j], slot_in.at[mine, me], j, me).start()
        shard_copy(HOTG, hotg_src, hotg_in.at[me], j, me).start()

    peers(send_grads)
    slot_in[mine, me] = slot_src[me]
    hotg_in[me] = hotg_src[...]

    dp_peers(lambda d: dp_copy(DIDS, idg.at[mine], idg.at[d], d, d).wait_recv())
    if keep_all:
        dp_peers(lambda d: fill(d, d))

    peers(lambda j: shard_copy(COLDG, slot_src.at[j], slot_in.at[mine, j], j, j).wait_recv())
    dp_peers(lambda d: dp_copy(DCOLD, slot_in.at[mine], slot_in.at[mine], d, mine).start())
    peers(lambda j: shard_copy(HOTG, hotg_src, hotg_in.at[j], j, j).wait_recv())
    hot_in[mine] = dot(hot_counts[...], hotg_in[...].reshape(group, embed)).astype(BF16)
    dp_peers(lambda d: dp_copy(DHOT, hot_in.at[mine], hot_in.at[mine], d, mine).start())

    def add_cold(d):
        where = d
        if not keep_all:
            fill(d, 0)
            where = 0
        gacc[...] += dot_tn(slot_in[d].reshape(slots, embed), onehot[where])

    gacc[...] = jnp.zeros_like(gacc)
    add_cold(mine)

    logits = jnp.zeros((8, samples), F32)

    def add_logit(i, total):
        j = lax.rem(me + i, n)

        @pl.when(i > 0)
        def _():
            shard_copy(LOGIT, logit_src.at[j], logit_in.at[j], j, j).wait_recv()

        return total + logit_in[j]

    logit_out[...] = lax.fori_loop(0, n, add_logit, logits)

    weight_out[...] = weight_in[mine].astype(F32)

    def add_weight(d):
        dp_copy(DWEIGHT, weight_in.at[mine], weight_in.at[d], d, d).wait_recv()
        weight_out[...] += weight_in[d].astype(F32)

    dp_peers(add_weight)

    def cold_from(d):
        dp_copy(DCOLD, slot_in.at[mine], slot_in.at[d], d, d).wait_recv()
        add_cold(d)

    dp_peers(cold_from)
    cold_out[...] = gacc[...].T.astype(BF16)

    def hot_from(i, total):
        d = lax.rem(mine + i, groups)

        @pl.when(i > 0)
        def _():
            dp_copy(DHOT, hot_in.at[mine], hot_in.at[d], d, d).wait_recv()

        return total + hot_in[d].astype(F32)

    hot_out[...] = lax.fori_loop(0, groups, hot_from, jnp.zeros((kept, embed), F32)).astype(BF16)

    def sent(j):
        shard_copy(IDS, ids_ref, idg.at[mine, me], j, me).wait_send()
        shard_copy(COT, cot_ref, cotg.at[me], j, me).wait_send()
        shard_copy(HOTIN, hot_src, ing.at[me, :, pl.ds(0, embed)], j, me).wait_send()
        shard_copy(ROWS, rows_src.at[j], answer.at[me], j, me).wait_send()
        shard_copy(COLDIN, cold_src, ing.at[me, :, pl.ds(embed, embed)], j, me).wait_send()
        shard_copy(PART, part_src.at[j], part_in.at[me], j, me).wait_send()
        shard_copy(LOGIT, logit_src.at[j], logit_in.at[me], j, me).wait_send()
        shard_copy(COLDG, slot_src.at[j], slot_in.at[mine, me], j, me).wait_send()
        shard_copy(HOTG, hotg_src, hotg_in.at[me], j, me).wait_send()

    peers(sent)

    def dp_sent(d):
        dp_copy(DIDS, idg.at[mine], idg.at[mine], d, mine).wait_send()
        dp_copy(DWEIGHT, weight_in.at[mine], weight_in.at[mine], d, mine).wait_send()
        dp_copy(DCOLD, slot_in.at[mine], slot_in.at[mine], d, mine).wait_send()
        dp_copy(DHOT, hot_in.at[mine], hot_in.at[mine], d, mine).wait_send()

    dp_peers(dp_sent)


def shards(
    hot_ids, cold_owner, cold_offset, hot_table, cold_table, w_in, bias_in, w_out, cotangent
):
    n = lax.axis_size("shard")
    groups = lax.axis_size("dp")
    samples, width = hot_ids.shape
    table_rows, embed = hot_table.shape
    owned = cold_table.shape[0]
    inputs_dim, hidden_dev = w_in.shape
    lookups = cold_offset.shape[0]
    cap = max(16, 2 * lookups // n)
    kept = table_rows // n
    slots = n * cap
    keep_all = groups * slots * owned * 2 <= 20 * 2**20
    owner_rows = cold_owner.reshape(samples, 2).T
    offset_rows = cold_offset.reshape(samples, 2).T
    ids = jnp.concatenate(
        [hot_ids.T, owner_rows, offset_rows, jnp.zeros((12 - width, samples), I32)], axis=0
    )
    cot = jnp.broadcast_to(cotangent[None, :], (8, samples))
    vmem = pl.BlockSpec(memory_space=pltpu.VMEM)
    logits, hot, cold, weight = pl.pallas_call(
        functools.partial(kernel, n, groups, cap, keep_all),
        out_shape=(
            jax.ShapeDtypeStruct((8, samples), F32),
            jax.ShapeDtypeStruct((kept, embed), BF16),
            jax.ShapeDtypeStruct((owned, embed), BF16),
            jax.ShapeDtypeStruct((inputs_dim, hidden_dev), F32),
        ),
        in_specs=[vmem] * 8,
        out_specs=(vmem,) * 4,
        scratch_shapes=[
            pltpu.VMEM((groups, n, 16, samples), I32),
            pltpu.VMEM((n, 8, samples), F32),
            pltpu.VMEM((n, samples, 2 * embed), BF16),
            pltpu.VMEM((samples, embed), BF16),
            pltpu.VMEM((samples, embed), BF16),
            pltpu.VMEM((slots, samples), BF16),
            pltpu.VMEM((lookups, lookups), BF16),
            pltpu.VMEM((slots, embed), I32),
            pltpu.VMEM((groups if keep_all else 1, slots, owned), BF16),
            pltpu.VMEM((n, cap, embed), BF16),
            pltpu.VMEM((n, cap, embed), BF16),
            pltpu.VMEM((kept, n * samples), BF16),
            pltpu.VMEM((n, samples, hidden_dev), BF16),
            pltpu.VMEM((n, samples, 2 * embed), BF16),
            pltpu.VMEM((n, samples, 2 * embed), BF16),
            pltpu.VMEM((n, 8, samples), F32),
            pltpu.VMEM((n, 8, samples), F32),
            pltpu.VMEM((n, cap, embed), BF16),
            pltpu.VMEM((groups, n, cap, embed), BF16),
            pltpu.VMEM((samples, embed), BF16),
            pltpu.VMEM((n, samples, embed), BF16),
            pltpu.VMEM((groups, inputs_dim, hidden_dev), BF16),
            pltpu.VMEM((groups, kept, embed), BF16),
            pltpu.VMEM((embed, owned), F32),
            pltpu.SemaphoreType.DMA((9, n)),
            pltpu.SemaphoreType.DMA((9, n)),
            pltpu.SemaphoreType.DMA((4, groups)),
            pltpu.SemaphoreType.DMA((4, groups)),
        ],
        compiler_params=pltpu.CompilerParams(
            collective_id=0, has_side_effects=True, vmem_limit_bytes=56 * 2**20
        ),
    )(ids, hot_ids, cot, hot_table, cold_table, w_in, bias_in, w_out)
    return (logits[0], hot, cold, weight)


def solution(mesh):
    in_specs = (
        P(("dp", "shard"), None),
        P(("dp", "shard"), None),
        P(("dp", "shard")),
        P(),
        P("shard", None),
        P(None, "shard"),
        P(None, "shard"),
        P(None, "shard"),
        P(("dp", "shard")),
    )
    out_specs = (P(("dp", "shard")), P("shard", None), P("shard", None), P(None, "shard"))
    return jax.shard_map(shards, mesh=mesh, in_specs=in_specs, out_specs=out_specs, check_vma=False)
```

time: 216 us -> 82.6 us (0.38)
  the two profiles are of different devices: /device:TPU:0 before, /device:TPU:29 now
where the time goes in v1:
time: 82.6 us; the launch traced here: 82.3 us
  Pallas kernels  70.1 us (85%)
  local copies, waits for them, and re-layouts  10.2 us (12%)
  other arithmetic  1.33 us (2%)
    pallas_call x1, Pallas kernels, shards(): pl.pallas_call(functools.partial(kernel, n, groups, cap, keep_all), out_s...  70.1 us
    unnamed x15, local copies, waits for them, and re-layouts  7.98 us

profile of v1, /device:TPU:29, one launch (start us, length us, event | category | flops | bytes accessed | tf_op | source)
XLA Modules:
  0.0 82.3 jit_solution(2483321583869565003)
XLA Ops:
  0.6 0.0 copy-start.3
  0.6 0.5 broadcast.6
  1.2 0.2 copy-done.3
  1.3 0.7 reduce.3
  2.0 0.0 copy-start.4
  2.0 0.1 pad.3.clone
  2.1 0.6 copy-done.4
  2.6 0.6 broadcast_in_dim.10.cot_ref
  3.2 0.1 reshape.15
  3.4 0.1 copy.14
  3.4 0.0 copy-start.2
  3.4 0.7 copy-done.2
  4.1 0.1 reshape.16
  4.3 0.0 copy-start.1
  4.3 0.1 copy.15
  4.4 0.6 copy-done.1
  5.0 0.7 add_add_fusion.ids_ref
  5.6 0.7 copy.16.hot_col
  6.4 70.1 %shard_map.120 = (f32[8,128]{1,0:T(8,128)}, bf16[512,128]{1,0:T(8,128)(2,1)}, bf16[4096,128]{1,0:T(8,128)(2,1)}, f32[256,512]{1,0:T(8,128)}) custom-call(s32[16,128]{1,0:T(8,128)} %add_add_fusion.ids_ref, s32[128,8]{1,0:T(8,128)} %copy.16.hot_col, f32[8,128]{1,0:T(8,128)} %broadcast_in_dim.10.cot_ref, bf16[4096,128]{1,0:T(8,128)(2,1)} %hot_table.1, ...), custom_call_target="tpu_custom_call" | custom-call | tf_op jit(solution)/shard_map/pallas_call | solution.py:321
  76.4 1.2 %slice_bitcast_fusion = f32[128]{0:T(128)} fusion(f32[8,128]{1,0:T(8,128)} %get-tuple-element.8), kind=kLoop, calls=%fused_computation.1 | loop fusion | bytes 1024 | tf_op jit(solution)/shard_map/squeeze | solution.py:365
  77.6 1.6 %copy.20 = bf16[512,128]{1,0:T(8,128)(2,1)} copy(bf16[512,128]{1,0:T(8,128)(2,1)} %get-tuple-element.17) | data formatting | bytes 262144
  79.2 0.0 copy-start
  79.2 2.3 %copy.21 = bf16[4096,128]{1,0:T(8,128)(2,1)} copy(bf16[4096,128]{1,0:T(8,128)(2,1)} %get-tuple-element.18) | data formatting | bytes 2097152
  81.5 0.0 copy-done
  81.5 0.8 copy.22
  (1 shorter events, 0.0 us)
Async XLA Ops:
  0.6 0.7 copy-start.3
  2.0 0.7 copy-start.4
  3.4 0.7 copy-start.2
  4.3 0.7 copy-start.1
  79.2 2.3 %copy-start = (f32[256,512]{1,0:T(8,128)S(1)}, f32[256,512]{1,0:T(8,128)}, u32[]{:S(2)}) copy-start(f32[256,512]{1,0:T(8,128)} %get-tuple-element.19) | copy-start | bytes 1572868

commit v2 on v1

--- a/solution.py
+++ b/solution.py
@@ -26,16 +26,17 @@
 
 def kernel(
     n, groups, cap, keep_all,
-    ids_ref, hot_col, cot_ref, hot_table, cold_table, w_in, bias, w_out,
+    hot_rows, owner_ref, offset_ref, cot_row, hot_table, cold_table, w_in, bias, w_out,
     logit_out, hot_out, cold_out, weight_out,
-    idg, cotg, ing, hot_src, cold_src, pick, tri, offc, onehot, rows_src, answer,
+    ids_ref, cot_ref, hot_col, idg, cotg, ing, hot_src, cold_src, pick, tri, offc, onehot, turned,
+    rows_src, answer,
     hot_counts, grads, part_src, part_in, logit_src, logit_in, slot_src, slot_in,
     hotg_src, hotg_in, weight_in, hot_in, gacc,
     ssem, rsem, dssem, drsem,
 ):
     me = lax.axis_index("shard")
     mine = lax.axis_index("dp")
-    samples, width = hot_col.shape
+    width, samples = hot_rows.shape
     table_rows, embed = hot_table.shape
     owned = cold_table.shape[0]
     hidden_dev = w_in.shape[1]
@@ -67,6 +68,12 @@
     def dp_peers(body):
         peers(body, groups, mine)
 
+    ids_ref[0:width] = hot_rows[...]
+    ids_ref[width : width + 2] = owner_ref[...]
+    ids_ref[width + 2 : width + 4] = offset_ref[...]
+    ids_ref[width + 4 : 16] = jnp.zeros((12 - width, samples), I32)
+    cot_ref[...] = jnp.broadcast_to(cot_row[...], (8, samples))
+
     barrier = pltpu.get_barrier_semaphore()
     peers(lambda j: pl.semaphore_signal(
         barrier, inc=1, device_id={"shard": j}, device_id_type=pl.DeviceIdType.MESH))
@@ -82,6 +89,8 @@
     idg[mine, me] = ids_ref[...]
     cotg[me] = cot_ref[...]
 
+    spare = jnp.zeros((samples - width, samples), F32)
+    hot_col[...] = jnp.concatenate([hot_rows[...].astype(F32), spare], axis=0).T.astype(I32)
     chunk = min(512, table_rows)
     pooled = jnp.zeros((samples, embed), F32)
     lane = lax.broadcasted_iota(I32, (samples, chunk), 1)
@@ -107,42 +116,49 @@
     match = jnp.where(lax.broadcasted_iota(I32, (n, lookups), 0) == owner, 1.0, 0.0)
     order = dot(match.astype(BF16), tri[...])
     place = owner * cap + jnp.sum(match * order, axis=0, keepdims=True).astype(I32)
-    slot_i = lax.broadcasted_iota(I32, (slots, samples), 0)
-    pick[...] = (
-        jnp.where(slot_i == place[:, :samples], 1.0, 0.0)
-        + jnp.where(slot_i == place[:, samples:], 1.0, 0.0)
-    ).astype(BF16)
+    slot_i = lax.broadcasted_iota(I32, (slots, lookups), 0)
+    first = 2 * lax.broadcasted_iota(I32, (lookups, samples), 1)
+    lookup_i = lax.broadcasted_iota(I32, (lookups, samples), 0)
+    pair = jnp.where((lookup_i == first) | (lookup_i == first + 1), 1.0, 0.0).astype(BF16)
+    pick[...] = dot(jnp.where(slot_i == place, 1.0, 0.0).astype(BF16), pair).astype(BF16)
 
     cap_i = lax.broadcasted_iota(I32, (cap, lookups), 0)
 
-    def fill(d, place_at):
-        def one(j, carry):
-            block = idg[d, j]
-            hit = jnp.where(lookup_rows(block, width) == me, 1.0, 0.0)
-            spread = jnp.broadcast_to(hit, (16, lookups))
-            position = dot(spread.astype(BF16), tri[...])[0:1].astype(I32)
-            chosen = jnp.where(cap_i == position, hit, 0.0).astype(BF16)
-            offset = lookup_rows(block, width + 2)
+    def find(d):
+        hits = [jnp.where(lookup_rows(idg[d, j], width) == me, 1.0, 0.0) for j in range(n)]
+        positions = dot(jnp.concatenate(hits, axis=0).astype(BF16), tri[...]).astype(I32)
+        for j in range(n):
+            chosen = jnp.where(cap_i == positions[j : j + 1], hits[j], 0.0).astype(BF16)
+            offset = lookup_rows(idg[d, j], width + 2)
             high = jnp.broadcast_to((offset >> 6).astype(F32), (embed, lookups)).astype(BF16)
             low = jnp.broadcast_to((offset & 63).astype(F32), (embed, lookups)).astype(BF16)
-            found = dot_nt(chosen, high) * 64.0 + dot_nt(chosen, low)
-            offc[pl.ds(pl.multiple_of(j * cap, cap), cap), :] = found.astype(I32)
-            return carry
-
-        lax.fori_loop(0, n, one, 0)
-        lanes = lax.broadcasted_iota(I32, (slots, embed), 1)
-        for c in range(owned // embed):
-            onehot[place_at, :, c * embed : (c + 1) * embed] = jnp.where(
-                offc[...] - c * embed == lanes, 1.0, 0.0
+            offc[j * cap : (j + 1) * cap, :] = dot_nt(chosen, high) * 64.0 + dot_nt(chosen, low)
+
+    tall = 64
+
+    def turn(place_at):
+        row = offc[...].T[0:1].astype(I32)
+        down = lax.broadcasted_iota(I32, (tall, slots), 0)
+        for c in range(owned // tall):
+            turned[place_at, c * tall : (c + 1) * tall, :] = jnp.where(
+                row - c * tall == down, 1.0, 0.0
             ).astype(BF16)
 
     peers(lambda j: shard_copy(IDS, ids_ref, idg.at[mine, j], j, j).wait_recv())
     dp_peers(lambda d: dp_copy(DIDS, idg.at[mine], idg.at[mine], d, mine).start())
-    at = mine if keep_all else 0
-    fill(mine, at)
-    rows_src[...] = dot(onehot[at], cold_table[...]).astype(BF16).reshape(n, cap, embed)
+    find(mine)
+    across = lax.broadcasted_iota(I32, (slots, embed), 1)
+    offsets = offc[...].astype(I32)
+    for c in range(owned // embed):
+        onehot[:, c * embed : (c + 1) * embed] = jnp.where(
+            offsets - c * embed == across, 1.0, 0.0
+        ).astype(BF16)
+    rows_src[...] = dot(onehot[...], cold_table[...]).astype(BF16).reshape(n, cap, embed)
     peers(lambda j: shard_copy(ROWS, rows_src.at[j], answer.at[me], j, me).start())
     answer[me] = rows_src[me]
+
+    if keep_all:
+        turn(mine)
 
     kept_i = lax.broadcasted_iota(I32, (kept, samples), 0) + me * kept
     for j in range(n):
@@ -155,6 +171,20 @@
     cold_src[...] = dot_tn(pick[...], answer[...].reshape(slots, embed)).astype(BF16)
     peers(lambda j: shard_copy(COLDIN, cold_src, ing.at[me, :, pl.ds(embed, embed)], j, me).start())
     ing[me, :, embed : 2 * embed] = cold_src[...]
+
+    def other_tables(low, high):
+        def step(i, carry):
+            d = lax.rem(mine + groups - i, groups)
+            dp_copy(DIDS, idg.at[mine], idg.at[d], d, d).wait_recv()
+            if keep_all:
+                find(d)
+                turn(d)
+            return carry
+
+        lax.fori_loop(low, high, step, 0)
+
+    half = 1 + groups // 2
+    other_tables(1, half)
 
     head_rows = jnp.broadcast_to(w_out[...], (16, hidden_dev))
 
@@ -194,6 +224,8 @@
     ).astype(BF16)
     dp_peers(lambda d: dp_copy(DWEIGHT, weight_in.at[mine], weight_in.at[mine], d, mine).start())
 
+    other_tables(half, groups)
+
     def add_part(i, total):
         j = lax.rem(me + i, n)
 
@@ -215,10 +247,6 @@
     peers(send_grads)
     slot_in[mine, me] = slot_src[me]
     hotg_in[me] = hotg_src[...]
-
-    dp_peers(lambda d: dp_copy(DIDS, idg.at[mine], idg.at[d], d, d).wait_recv())
-    if keep_all:
-        dp_peers(lambda d: fill(d, d))
 
     peers(lambda j: shard_copy(COLDG, slot_src.at[j], slot_in.at[mine, j], j, j).wait_recv())
     dp_peers(lambda d: dp_copy(DCOLD, slot_in.at[mine], slot_in.at[mine], d, mine).start())
@@ -229,9 +257,10 @@
     def add_cold(d):
         where = d
         if not keep_all:
-            fill(d, 0)
+            find(d)
+            turn(0)
             where = 0
-        gacc[...] += dot_tn(slot_in[d].reshape(slots, embed), onehot[where])
+        gacc[...] += dot(turned[where], slot_in[d].reshape(slots, embed))
 
     gacc[...] = jnp.zeros_like(gacc)
     add_cold(mine)
@@ -247,7 +276,7 @@
 
         return total + logit_in[j]
 
-    logit_out[...] = lax.fori_loop(0, n, add_logit, logits)
+    logit_out[...] = lax.fori_loop(0, n, add_logit, logits)[0:1]
 
     weight_out[...] = weight_in[mine].astype(F32)
 
@@ -262,7 +291,7 @@
         add_cold(d)
 
     dp_peers(cold_from)
-    cold_out[...] = gacc[...].T.astype(BF16)
+    cold_out[...] = gacc[...].astype(BF16)
 
     def hot_from(i, total):
         d = lax.rem(mine + i, groups)
@@ -302,7 +331,7 @@
 ):
     n = lax.axis_size("shard")
     groups = lax.axis_size("dp")
-    samples, width = hot_ids.shape
+    samples = hot_ids.shape[0]
     table_rows, embed = hot_table.shape
     owned = cold_table.shape[0]
     inputs_dim, hidden_dev = w_in.shape
@@ -311,24 +340,21 @@
     kept = table_rows // n
     slots = n * cap
     keep_all = groups * slots * owned * 2 <= 20 * 2**20
-    owner_rows = cold_owner.reshape(samples, 2).T
-    offset_rows = cold_offset.reshape(samples, 2).T
-    ids = jnp.concatenate(
-        [hot_ids.T, owner_rows, offset_rows, jnp.zeros((12 - width, samples), I32)], axis=0
-    )
-    cot = jnp.broadcast_to(cotangent[None, :], (8, samples))
     vmem = pl.BlockSpec(memory_space=pltpu.VMEM)
     logits, hot, cold, weight = pl.pallas_call(
         functools.partial(kernel, n, groups, cap, keep_all),
         out_shape=(
-            jax.ShapeDtypeStruct((8, samples), F32),
+            jax.ShapeDtypeStruct((1, samples), F32),
             jax.ShapeDtypeStruct((kept, embed), BF16),
             jax.ShapeDtypeStruct((owned, embed), BF16),
             jax.ShapeDtypeStruct((inputs_dim, hidden_dev), F32),
         ),
-        in_specs=[vmem] * 8,
+        in_specs=[vmem] * 9,
         out_specs=(vmem,) * 4,
         scratch_shapes=[
+            pltpu.VMEM((16, samples), I32),
+            pltpu.VMEM((8, samples), F32),
+            pltpu.VMEM((samples, samples), I32),
             pltpu.VMEM((groups, n, 16, samples), I32),
             pltpu.VMEM((n, 8, samples), F32),
             pltpu.VMEM((n, samples, 2 * embed), BF16),
@@ -336,8 +362,9 @@
             pltpu.VMEM((samples, embed), BF16),
             pltpu.VMEM((slots, samples), BF16),
             pltpu.VMEM((lookups, lookups), BF16),
-            pltpu.VMEM((slots, embed), I32),
-            pltpu.VMEM((groups if keep_all else 1, slots, owned), BF16),
+            pltpu.VMEM((slots, embed), F32),
+            pltpu.VMEM((slots, owned), BF16),
+            pltpu.VMEM((groups if keep_all else 1, owned, slots), BF16),
             pltpu.VMEM((n, cap, embed), BF16),
             pltpu.VMEM((n, cap, embed), BF16),
             pltpu.VMEM((kept, n * samples), BF16),
@@ -352,7 +379,7 @@
             pltpu.VMEM((n, samples, embed), BF16),
             pltpu.VMEM((groups, inputs_dim, hidden_dev), BF16),
             pltpu.VMEM((groups, kept, embed), BF16),
-            pltpu.VMEM((embed, owned), F32),
+            pltpu.VMEM((owned, embed), F32),
             pltpu.SemaphoreType.DMA((9, n)),
             pltpu.SemaphoreType.DMA((9, n)),
             pltpu.SemaphoreType.DMA((4, groups)),
@@ -361,8 +388,11 @@
         compiler_params=pltpu.CompilerParams(
             collective_id=0, has_side_effects=True, vmem_limit_bytes=56 * 2**20
         ),
-    )(ids, hot_ids, cot, hot_table, cold_table, w_in, bias_in, w_out)
-    return (logits[0], hot, cold, weight)
+    )(
+        hot_ids.T, cold_owner.reshape(2, samples), cold_offset.reshape(2, samples),
+        cotangent.reshape(1, samples), hot_table, cold_table, w_in, bias_in, w_out,
+    )
+    return (logits.reshape(samples), hot, cold, weight)
 
 
 def solution(mesh):

time: 82.6 us -> 73.3 us (0.89)
  the two profiles are of different devices: /device:TPU:29 before, /device:TPU:0 now
where the time goes in v2:
time: 73.3 us; the launch traced here: 73.1 us
  Pallas kernels  66.6 us (91%)
  local copies, waits for them, and re-layouts  5.76 us (8%)
    pallas_call x1, Pallas kernels, shards(): pl.pallas_call(functools.partial(kernel, n, groups, cap, keep_all), out_s...  66.6 us
    unnamed x8, local copies, waits for them, and re-layouts  5.76 us

profile of v2, /device:TPU:0, one launch (start us, length us, event | category | flops | bytes accessed | tf_op | source)
XLA Modules:
  0.0 73.1 jit_solution(13449982496411417495)
XLA Ops:
  0.6 66.6 %shard_map.120 = (f32[1,128]{1,0:T(1,128)}, bf16[512,128]{1,0:T(8,128)(2,1)}, bf16[4096,128]{1,0:T(8,128)(2,1)}, f32[256,512]{1,0:T(8,128)}) custom-call(s32[8,128]{1,0:T(8,128)} %bitcast.5, s32[2,128]{1,0:T(2,128)} %bitcast.6, s32[2,128]{1,0:T(2,128)} %bitcast.7, f32[1,128]{1,0:T(1,128)} %bitcast.8, bf16[4096,128]{1,0:T(8,128)(2,1)} %hot_table.1, ...), custom_call_target="tpu_custom_call" | custom-call | tf_op jit(solution)/shard_map/pallas_call | solution.py:344
  67.3 0.0 copy-start.1
  67.3 0.6 copy-done.1
  67.9 0.5 copy.17
  68.4 1.6 %copy.18 = bf16[512,128]{1,0:T(8,128)(2,1)} copy(bf16[512,128]{1,0:T(8,128)(2,1)} %get-tuple-element.17) | data formatting | bytes 262144
  69.9 0.0 copy-start
  69.9 2.3 %copy.19 = bf16[4096,128]{1,0:T(8,128)(2,1)} copy(bf16[4096,128]{1,0:T(8,128)(2,1)} %get-tuple-element.18) | data formatting | bytes 2097152
  72.3 0.0 copy-done
  72.3 0.8 %copy.20 = f32[256,512]{1,0:T(8,128)} copy(f32[256,512]{1,0:T(8,128)S(1)} %copy-done) | data formatting | bytes 1048576
Async XLA Ops:
  67.3 0.6 copy-start.1
  69.9 2.3 %copy-start = (f32[256,512]{1,0:T(8,128)S(1)}, f32[256,512]{1,0:T(8,128)}, u32[]{:S(2)}) copy-start(f32[256,512]{1,0:T(8,128)} %get-tuple-element.19) | copy-start | bytes 1572868

commit v3 on v2

--- a/solution.py
+++ b/solution.py
@@ -68,6 +68,40 @@
     def dp_peers(body):
         peers(body, groups, mine)
 
+    sibling = me + 1 - 2 * lax.rem(me, 2)
+
+    def same_core(body):
+        def step(i, carry):
+            body(lax.rem(me + n - 2 * i, n))
+            return carry
+
+        lax.fori_loop(1, n // 2, step, 0)
+
+    def gather_start(phase, src, view):
+        same_core(lambda j: shard_copy(phase, src, view(me), j, me).start())
+        shard_copy(phase, src, view(me), sibling, me).start()
+
+    def gather_pass(phase, src, view):
+        def one(j):
+            shard_copy(phase, src, view(j), j, j).wait_recv()
+            other = j + 1 - 2 * lax.rem(j, 2)
+            pltpu.make_async_remote_copy(
+                src_ref=view(j), dst_ref=view(j), send_sem=ssem.at[phase, other],
+                recv_sem=rsem.at[phase, j], device_id={"shard": sibling},
+                device_id_type=pl.DeviceIdType.MESH,
+            ).start()
+
+        same_core(one)
+
+    def hot_view(j):
+        return ing.at[j, :, pl.ds(0, embed)]
+
+    def cold_view(j):
+        return ing.at[j, :, pl.ds(embed, embed)]
+
+    def grad_view(j):
+        return hotg_in.at[j]
+
     ids_ref[0:width] = hot_rows[...]
     ids_ref[width : width + 2] = owner_ref[...]
     ids_ref[width + 2 : width + 4] = offset_ref[...]
@@ -100,7 +134,7 @@
             count = count + jnp.where(hot_col[:, k : k + 1] - c * chunk == lane, 1.0, 0.0)
         pooled = pooled + dot(count.astype(BF16), hot_table[c * chunk : (c + 1) * chunk, :])
     hot_src[...] = pooled.astype(BF16)
-    peers(lambda j: shard_copy(HOTIN, hot_src, ing.at[me, :, pl.ds(0, embed)], j, me).start())
+    gather_start(HOTIN, hot_src, hot_view)
     ing[me, :, 0:embed] = hot_src[...]
 
     lookups = 2 * samples
@@ -156,6 +190,7 @@
     rows_src[...] = dot(onehot[...], cold_table[...]).astype(BF16).reshape(n, cap, embed)
     peers(lambda j: shard_copy(ROWS, rows_src.at[j], answer.at[me], j, me).start())
     answer[me] = rows_src[me]
+    gather_pass(HOTIN, hot_src, hot_view)
 
     if keep_all:
         turn(mine)
@@ -169,7 +204,7 @@
 
     peers(lambda j: shard_copy(ROWS, rows_src.at[j], answer.at[j], j, j).wait_recv())
     cold_src[...] = dot_tn(pick[...], answer[...].reshape(slots, embed)).astype(BF16)
-    peers(lambda j: shard_copy(COLDIN, cold_src, ing.at[me, :, pl.ds(embed, embed)], j, me).start())
+    gather_start(COLDIN, cold_src, cold_view)
     ing[me, :, embed : 2 * embed] = cold_src[...]
 
     def other_tables(low, high):
@@ -184,17 +219,22 @@
         lax.fori_loop(low, high, step, 0)
 
     half = 1 + groups // 2
-    other_tables(1, half)
+    other_tables(1, 2)
+    gather_pass(COLDIN, cold_src, cold_view)
+    other_tables(2, half)
 
     head_rows = jnp.broadcast_to(w_out[...], (16, hidden_dev))
 
     def dense(i, carry):
         j = lax.rem(me + i, n)
 
-        @pl.when(i > 0)
+        @pl.when(lax.rem(i, 2) == 1)
         def _():
             shard_copy(HOTIN, hot_src, ing.at[j, :, pl.ds(0, embed)], j, j).wait_recv()
             shard_copy(COLDIN, cold_src, ing.at[j, :, pl.ds(embed, embed)], j, j).wait_recv()
+
+        @pl.when(i > 0)
+        def _():
             shard_copy(COT, cot_ref, cotg.at[j], j, j).wait_recv()
 
         pre = dot(ing[j], w_in[...]) + bias[...].astype(F32)
@@ -242,15 +282,22 @@
 
     def send_grads(j):
         shard_copy(COLDG, slot_src.at[j], slot_in.at[mine, me], j, me).start()
-        shard_copy(HOTG, hotg_src, hotg_in.at[me], j, me).start()
 
     peers(send_grads)
+    gather_start(HOTG, hotg_src, grad_view)
     slot_in[mine, me] = slot_src[me]
     hotg_in[me] = hotg_src[...]
+    gather_pass(HOTG, hotg_src, grad_view)
 
     peers(lambda j: shard_copy(COLDG, slot_src.at[j], slot_in.at[mine, j], j, j).wait_recv())
     dp_peers(lambda d: dp_copy(DCOLD, slot_in.at[mine], slot_in.at[mine], d, mine).start())
-    peers(lambda j: shard_copy(HOTG, hotg_src, hotg_in.at[j], j, j).wait_recv())
+    shard_copy(HOTG, hotg_src, hotg_in.at[sibling], sibling, sibling).wait_recv()
+
+    def handed(j):
+        other = j + 1 - 2 * lax.rem(j, 2)
+        shard_copy(HOTG, hotg_src, hotg_in.at[other], other, other).wait_recv()
+
+    same_core(handed)
     hot_in[mine] = dot(hot_counts[...], hotg_in[...].reshape(group, embed)).astype(BF16)
     dp_peers(lambda d: dp_copy(DHOT, hot_in.at[mine], hot_in.at[mine], d, mine).start())
 

time: 73.3 us -> 69.2 us (0.944)
  Pallas kernels: 66.6 us -> 62.6 us
    pallas_call x1, Pallas kernels: 66.6 us -> 62.6 us  [shards(): pl.pallas_call(functools.partial(kernel, n, groups, cap, keep_all), out_s...]
where the time goes in v3:
time: 69.2 us; the launch traced here: 69 us
  Pallas kernels  62.6 us (90%)
  local copies, waits for them, and re-layouts  5.76 us (8%)
    pallas_call x1, Pallas kernels, shards(): pl.pallas_call(functools.partial(kernel, n, groups, cap, keep_all), out_s...  62.6 us
    unnamed x8, local copies, waits for them, and re-layouts  5.76 us

profile of v3, /device:TPU:0, one launch (start us, length us, event | category | flops | bytes accessed | tf_op | source)
XLA Modules:
  0.0 69.0 jit_solution(1982566092917771709)
XLA Ops:
  0.6 62.6 %shard_map.120 = (f32[1,128]{1,0:T(1,128)}, bf16[512,128]{1,0:T(8,128)(2,1)}, bf16[4096,128]{1,0:T(8,128)(2,1)}, f32[256,512]{1,0:T(8,128)}) custom-call(s32[8,128]{1,0:T(8,128)} %bitcast.5, s32[2,128]{1,0:T(2,128)} %bitcast.6, s32[2,128]{1,0:T(2,128)} %bitcast.7, f32[1,128]{1,0:T(1,128)} %bitcast.8, bf16[4096,128]{1,0:T(8,128)(2,1)} %hot_table.1, ...), custom_call_target="tpu_custom_call" | custom-call | tf_op jit(solution)/shard_map/pallas_call | solution.py:391
  63.2 0.0 copy-start.1
  63.2 0.6 copy-done.1
  63.8 0.5 copy.17
  64.3 1.6 %copy.18 = bf16[512,128]{1,0:T(8,128)(2,1)} copy(bf16[512,128]{1,0:T(8,128)(2,1)} %get-tuple-element.17) | data formatting | bytes 262144
  65.9 0.0 copy-start
  65.9 2.3 %copy.19 = bf16[4096,128]{1,0:T(8,128)(2,1)} copy(bf16[4096,128]{1,0:T(8,128)(2,1)} %get-tuple-element.18) | data formatting | bytes 2097152
  68.2 0.0 copy-done
  68.2 0.8 %copy.20 = f32[256,512]{1,0:T(8,128)} copy(f32[256,512]{1,0:T(8,128)S(1)} %copy-done) | data formatting | bytes 1048576
Async XLA Ops:
  63.2 0.6 copy-start.1
  65.9 2.3 %copy-start = (f32[256,512]{1,0:T(8,128)S(1)}, f32[256,512]{1,0:T(8,128)}, u32[]{:S(2)}) copy-start(f32[256,512]{1,0:T(8,128)} %get-tuple-element.19) | copy-start | bytes 1572868
